TPU v7x, 128 devices: a whole 4x4x4 slice. The times are simulated.
128 devices in a mesh: lon: 8 (over y, core), lat: 16 (over z, x).
Axes of the slice: x: 4, y: 4, z: 4, core: 2. Of those that a mesh axis runs over, the one named last changes fastest.
Arguments:
- state: float32 [512, 4, 16, 2880], P('lat', None, None, 'lon'), may hold values from -6 to 6
- band: int32 [256], replicated, may hold values from 1 to 32, as said below
- damping: float32 [256], replicated, may hold values from 0.2 to 0.9
Outputs:
- advanced: float32 [512, 4, 16, 2880], P('lat', None, None, 'lon')
Inputs may be any that keep to these rules, and one draw needn't show every extreme that they name: Each polar latitude's band half width is an integer from 1 to 32; 32 is reached at some latitude.
All inputs are finite; a program needn't handle non-finite values.
Results may differ from a plain program's by a relative error of at most 0.00007.
Values sent between devices are 32-bit elements; how exact they have to be, the bound alone decides.
A program may use at most 128 MiB of HBM per device.

v0:
```python
import math
import jax
import jax.numpy as jnp
from jax import lax
from jax.sharding import PartitionSpec as P

MAXB = 32
KX = 0.004
KY = 0.1
FC = 0.2
GROUP = 5


def with_halo(cells, sides, width, closed):
    for axis, dim in sides:
        count = lax.axis_size(axis)
        ends = count if closed else count - 1
        head = lax.slice_in_dim(cells, 0, width, axis=dim)
        tail = lax.slice_in_dim(cells, cells.shape[dim] - width, cells.shape[dim], axis=dim)
        cells = jnp.concatenate(
            [
                lax.ppermute(tail, axis, [(i, (i + 1) % count) for i in range(ends)]),
                cells,
                lax.ppermute(head, axis, [((i + 1) % count, i) for i in range(ends)]),
            ],
            axis=dim,
        )
    return cells


def advance_cells(padded, cos_rows, sin_rows, cos_pad):
    u = padded[:, 0]
    v = padded[:, 1]
    h = padded[:, 2]
    q = padded[:, 3]
    inv = 1.0 / cos_rows[:, None, None]
    sn = sin_rows[:, None, None]
    cp = cos_pad[:, None, None]

    def middle(a):
        return a[1:-1, :, 1:-1]

    def east(a):
        return a[1:-1, :, 2:]

    def west(a):
        return a[1:-1, :, :-2]

    def north(a):
        return a[2:, :, 1:-1]

    def south(a):
        return a[:-2, :, 1:-1]

    flux_x = u * h
    flux_y = v * h * cp
    h_new = (
        middle(h)
        - KX * inv * (east(flux_x) - west(flux_x))
        - KY * inv * (north(flux_y) - south(flux_y))
    )
    u_new = middle(u) - KX * inv * (east(h) - west(h)) + FC * sn * middle(v)
    v_new = middle(v) - KY * (north(h) - south(h)) - FC * sn * middle(u)
    q_new = (
        middle(q)
        - KX * inv * middle(u) * (east(q) - west(q))
        - KY * middle(v) * (north(q) - south(q))
    )
    return jnp.stack([u_new, v_new, h_new, q_new], axis=1)


def tap_smooth(extended, width, length):
    taps = jnp.arange(-MAXB, MAXB + 1).astype(jnp.float32)
    weights = (
        jnp.maximum(width[:, None] + 1.0 - jnp.abs(taps)[None, :], 0.0)
        / (width[:, None] + 1.0) ** 2
    )
    start_shape = extended.shape[:3] + (length,)
    tap_count = 2 * MAXB + 1
    turns = tap_count // GROUP

    def add_one(tap, total):
        weight = lax.dynamic_index_in_dim(weights, tap, 1, keepdims=False)
        return total + weight[:, None, None, None] * lax.dynamic_slice_in_dim(
            extended, tap, length, 3
        )

    def add_group(step, total):
        for offset in range(GROUP):
            total = add_one(step * GROUP + offset, total)
        return total

    total = lax.fori_loop(0, turns, add_group, jnp.zeros(start_shape, jnp.float32))
    return total


def shards(state, band, damping):
    lon_count = lax.axis_size("lon")
    lat_count = lax.axis_size("lat")
    lat_rows, field_count, levels, lon_cells = state.shape
    lon_total = lon_cells * lon_count
    lat_total = lat_rows * lat_count
    polar_total = lat_total // 2
    quarter = lat_total // 4
    lon_place = lax.axis_index("lon")
    lat_place = lax.axis_index("lat")
    rimmed = with_halo(state, (("lon", 3),), 1, True)
    padded = with_halo(rimmed, (("lat", 0),), 1, False)
    rows = lat_place * lat_rows + jnp.arange(-1, lat_rows + 1, dtype=jnp.int32)
    angle = math.pi * ((rows.astype(jnp.float32) + 0.5) / lat_total - 0.5)
    cos_pad = jnp.cos(angle)
    stepped = advance_cells(padded, cos_pad[1:-1], jnp.sin(angle[1:-1]), cos_pad)
    band_float = band.astype(jnp.float32)

    def row_params(lats):
        is_polar = (lats < quarter) | (lats >= 3 * quarter)
        polar_place = jnp.where(lats < quarter, lats, lats - polar_total)
        onehot = (
            (polar_place[:, None] == jnp.arange(polar_total, dtype=jnp.int32)[None, :])
            & is_polar[:, None]
        ).astype(jnp.float32)
        width = jnp.dot(onehot, band_float, precision=lax.Precision.HIGHEST)
        strength = jnp.dot(onehot, damping, precision=lax.Precision.HIGHEST)
        return (width, strength)

    def damp_block(fields, lats):
        width, strength = row_params(lats)
        extended = jnp.concatenate([fields[..., -MAXB:], fields, fields[..., :MAXB]], axis=3)
        smooth = tap_smooth(extended, width, lon_total)
        return fields + strength[:, None, None, None] * (smooth - fields)

    gathered = lax.all_to_all(stepped, "lon", split_axis=0, concat_axis=3, tiled=True)
    part_rows = gathered.shape[0]
    spread = lax.all_to_all(gathered, "lat", split_axis=2, concat_axis=0, tiled=True)
    slots = jnp.arange(lat_count * part_rows, dtype=jnp.int32)
    lats = slots // part_rows * lat_rows + lon_place * part_rows + slots % part_rows
    edge = lat_count // 4 * part_rows
    southern = damp_block(spread[:edge], lats[:edge])
    northern = damp_block(spread[-edge:], lats[-edge:])
    spread = jnp.concatenate([southern, spread[edge:-edge], northern], axis=0)
    damped = lax.all_to_all(spread, "lat", split_axis=0, concat_axis=2, tiled=True)
    return lax.all_to_all(damped, "lon", split_axis=3, concat_axis=0, tiled=True)


def solution(mesh):
    in_specs = (P("lat", None, None, "lon"), P(), P())
    out_specs = P("lat", None, None, "lon")
    return jax.shard_map(shards, mesh=mesh, in_specs=in_specs, out_specs=out_specs, check_vma=False)
```

profile of v0, /device:TPU:1, one launch (start us, length us, event | category | flops | bytes accessed | tf_op | source)
XLA Modules:
  0.0 553.1 jit_solution(18015981450221543756)
XLA Ops:
  29.0 45.6 %all_to_all.69 = f32[32,4,16,360]{3,2,1,0:T(8,128)S(1)} all-to-all(f32[32,4,16,360]{3,2,1,0:T(8,128)S(1)} %pad_maximum_fusion.1), channel_id=1, replica_groups=mesh['lon'=8,'lat'=16] {'lon'}, dimensions={0} | all-to-all | bytes 5898240 | tf_op jit(solution)/shard_map/all_to_all | solution.py:132
  83.1 9.7 %all-to-all-start.1 = ((f32[4,4,16,2880]{3,1,0,2:T(4,128)}), f32[4,4,16,2880]{3,1,0,2:T(4,128)}, u32[]{:S(2)}, u32[]{:S(2)}) async-start(f32[4,4,16,2880]{3,1,0,2:T(4,128)} %copy.80), calls=%async_computation.1 | async-start | bytes 6029312 | tf_op jit(solution)/shard_map/all_to_all | solution.py:134
  94.0 42.7 %all-to-all-done.1 = f32[4,4,16,2880]{3,1,0,2:T(4,128)} async-done(((f32[4,4,16,2880]{3,1,0,2:T(4,128)}), f32[4,4,16,2880]{3,1,0,2:T(4,128)}, u32[]{:S(2)}, u32[]{:S(2)}) %all-to-all-start.1) | async-done | bytes 2949152 | tf_op jit(solution)/shard_map/all_to_all | solution.py:134
  145.2 115.6 %while.32 = (s32[]{:T(128)}, f32[16,4,1,2880]{3,2,1,0:T(1,128)S(1)}, f32[16,65]{0,1:T(8,128)S(1)}, f32[16,4,1,2944]{3,2,1,0:T(1,128)S(1)}, s32[]{:T(128)}, /*ind...) while((s32[]{:T(128)}, ...), condition=%wide.region_1.2_spmd.clone, body=%wide.region_0.1_spmd.clone.sunk | while | flops 2027553 | bytes 5162514 | solution.py:93
  145.3 8.8 %multiply_add_fusion.4 = f32[16,4,1,2880]{3,2,1,0:T(1,128)S(1)} fusion(f32[16,4,1,2944]{3,2,1,0:T(1,128)S(1)} %get-tuple-element.535, s32[]{:T(128)S(6)} %select_n.276, s32[]{:T(128)S(6)} %select_n.277, s32[]{:T(128)S(6)} %select_n.278, s32[]{:T(128)S(6)} %select_n.279, s32[]{:T(128)S(6)} %select_n.280, f32[16,4,1,2880]{3,2,1,0:T(1,128)S(1)} %get-tuple-element.513, ...), kind=kLoop, calls=%fused_computation.4.clone.1 | loop fusion | flops 2027520 | bytes 5161301 | tf_op jit(solution)/shard_map/while/body/eval_jaxpr/add | solution.py:84
  154.1 8.8 %multiply_add_fusion.4 = f32[16,4,1,2880]{3,2,1,0:T(1,128)S(1)} fusion(f32[16,4,1,2944]{3,2,1,0:T(1,128)S(1)} %get-tuple-element.535, s32[]{:T(128)S(6)} %select_n.276, s32[]{:T(128)S(6)} %select_n.277, s32[]{:T(128)S(6)} %select_n.278, s32[]{:T(128)S(6)} %select_n.279, s32[]{:T(128)S(6)} %select_n.280, f32[16,4,1,2880]{3,2,1,0:T(1,128)S(1)} %get-tuple-element.513, ...), kind=kLoop, calls=%fused_computation.4.clone.1 | loop fusion | flops 2027520 | bytes 5161301 | tf_op jit(solution)/shard_map/while/body/eval_jaxpr/add | solution.py:84
  163.0 8.8 %multiply_add_fusion.4 = f32[16,4,1,2880]{3,2,1,0:T(1,128)S(1)} fusion(f32[16,4,1,2944]{3,2,1,0:T(1,128)S(1)} %get-tuple-element.535, s32[]{:T(128)S(6)} %select_n.276, s32[]{:T(128)S(6)} %select_n.277, s32[]{:T(128)S(6)} %select_n.278, s32[]{:T(128)S(6)} %select_n.279, s32[]{:T(128)S(6)} %select_n.280, f32[16,4,1,2880]{3,2,1,0:T(1,128)S(1)} %get-tuple-element.513, ...), kind=kLoop, calls=%fused_computation.4.clone.1 | loop fusion | flops 2027520 | bytes 5161301 | tf_op jit(solution)/shard_map/while/body/eval_jaxpr/add | solution.py:84
  171.9 8.8 %multiply_add_fusion.4 = f32[16,4,1,2880]{3,2,1,0:T(1,128)S(1)} fusion(f32[16,4,1,2944]{3,2,1,0:T(1,128)S(1)} %get-tuple-element.535, s32[]{:T(128)S(6)} %select_n.276, s32[]{:T(128)S(6)} %select_n.277, s32[]{:T(128)S(6)} %select_n.278, s32[]{:T(128)S(6)} %select_n.279, s32[]{:T(128)S(6)} %select_n.280, f32[16,4,1,2880]{3,2,1,0:T(1,128)S(1)} %get-tuple-element.513, ...), kind=kLoop, calls=%fused_computation.4.clone.1 | loop fusion | flops 2027520 | bytes 5161301 | tf_op jit(solution)/shard_map/while/body/eval_jaxpr/add | solution.py:84
  180.8 8.8 %multiply_add_fusion.4 = f32[16,4,1,2880]{3,2,1,0:T(1,128)S(1)} fusion(f32[16,4,1,2944]{3,2,1,0:T(1,128)S(1)} %get-tuple-element.535, s32[]{:T(128)S(6)} %select_n.276, s32[]{:T(128)S(6)} %select_n.277, s32[]{:T(128)S(6)} %select_n.278, s32[]{:T(128)S(6)} %select_n.279, s32[]{:T(128)S(6)} %select_n.280, f32[16,4,1,2880]{3,2,1,0:T(1,128)S(1)} %get-tuple-element.513, ...), kind=kLoop, calls=%fused_computation.4.clone.1 | loop fusion | flops 2027520 | bytes 5161301 | tf_op jit(solution)/shard_map/while/body/eval_jaxpr/add | solution.py:84
  189.7 8.8 %multiply_add_fusion.4 = f32[16,4,1,2880]{3,2,1,0:T(1,128)S(1)} fusion(f32[16,4,1,2944]{3,2,1,0:T(1,128)S(1)} %get-tuple-element.535, s32[]{:T(128)S(6)} %select_n.276, s32[]{:T(128)S(6)} %select_n.277, s32[]{:T(128)S(6)} %select_n.278, s32[]{:T(128)S(6)} %select_n.279, s32[]{:T(128)S(6)} %select_n.280, f32[16,4,1,2880]{3,2,1,0:T(1,128)S(1)} %get-tuple-element.513, ...), kind=kLoop, calls=%fused_computation.4.clone.1 | loop fusion | flops 2027520 | bytes 5161301 | tf_op jit(solution)/shard_map/while/body/eval_jaxpr/add | solution.py:84
  198.6 8.8 %multiply_add_fusion.4 = f32[16,4,1,2880]{3,2,1,0:T(1,128)S(1)} fusion(f32[16,4,1,2944]{3,2,1,0:T(1,128)S(1)} %get-tuple-element.535, s32[]{:T(128)S(6)} %select_n.276, s32[]{:T(128)S(6)} %select_n.277, s32[]{:T(128)S(6)} %select_n.278, s32[]{:T(128)S(6)} %select_n.279, s32[]{:T(128)S(6)} %select_n.280, f32[16,4,1,2880]{3,2,1,0:T(1,128)S(1)} %get-tuple-element.513, ...), kind=kLoop, calls=%fused_computation.4.clone.1 | loop fusion | flops 2027520 | bytes 5161301 | tf_op jit(solution)/shard_map/while/body/eval_jaxpr/add | solution.py:84
  207.5 8.8 %multiply_add_fusion.4 = f32[16,4,1,2880]{3,2,1,0:T(1,128)S(1)} fusion(f32[16,4,1,2944]{3,2,1,0:T(1,128)S(1)} %get-tuple-element.535, s32[]{:T(128)S(6)} %select_n.276, s32[]{:T(128)S(6)} %select_n.277, s32[]{:T(128)S(6)} %select_n.278, s32[]{:T(128)S(6)} %select_n.279, s32[]{:T(128)S(6)} %select_n.280, f32[16,4,1,2880]{3,2,1,0:T(1,128)S(1)} %get-tuple-element.513, ...), kind=kLoop, calls=%fused_computation.4.clone.1 | loop fusion | flops 2027520 | bytes 5161301 | tf_op jit(solution)/shard_map/while/body/eval_jaxpr/add | solution.py:84
  216.4 8.8 %multiply_add_fusion.4 = f32[16,4,1,2880]{3,2,1,0:T(1,128)S(1)} fusion(f32[16,4,1,2944]{3,2,1,0:T(1,128)S(1)} %get-tuple-element.535, s32[]{:T(128)S(6)} %select_n.276, s32[]{:T(128)S(6)} %select_n.277, s32[]{:T(128)S(6)} %select_n.278, s32[]{:T(128)S(6)} %select_n.279, s32[]{:T(128)S(6)} %select_n.280, f32[16,4,1,2880]{3,2,1,0:T(1,128)S(1)} %get-tuple-element.513, ...), kind=kLoop, calls=%fused_computation.4.clone.1 | loop fusion | flops 2027520 | bytes 5161301 | tf_op jit(solution)/shard_map/while/body/eval_jaxpr/add | solution.py:84
  225.3 8.8 %multiply_add_fusion.4 = f32[16,4,1,2880]{3,2,1,0:T(1,128)S(1)} fusion(f32[16,4,1,2944]{3,2,1,0:T(1,128)S(1)} %get-tuple-element.535, s32[]{:T(128)S(6)} %select_n.276, s32[]{:T(128)S(6)} %select_n.277, s32[]{:T(128)S(6)} %select_n.278, s32[]{:T(128)S(6)} %select_n.279, s32[]{:T(128)S(6)} %select_n.280, f32[16,4,1,2880]{3,2,1,0:T(1,128)S(1)} %get-tuple-element.513, ...), kind=kLoop, calls=%fused_computation.4.clone.1 | loop fusion | flops 2027520 | bytes 5161301 | tf_op jit(solution)/shard_map/while/body/eval_jaxpr/add | solution.py:84
  234.2 8.8 %multiply_add_fusion.4 = f32[16,4,1,2880]{3,2,1,0:T(1,128)S(1)} fusion(f32[16,4,1,2944]{3,2,1,0:T(1,128)S(1)} %get-tuple-element.535, s32[]{:T(128)S(6)} %select_n.276, s32[]{:T(128)S(6)} %select_n.277, s32[]{:T(128)S(6)} %select_n.278, s32[]{:T(128)S(6)} %select_n.279, s32[]{:T(128)S(6)} %select_n.280, f32[16,4,1,2880]{3,2,1,0:T(1,128)S(1)} %get-tuple-element.513, ...), kind=kLoop, calls=%fused_computation.4.clone.1 | loop fusion | flops 2027520 | bytes 5161301 | tf_op jit(solution)/shard_map/while/body/eval_jaxpr/add | solution.py:84
  243.0 8.8 %multiply_add_fusion.4 = f32[16,4,1,2880]{3,2,1,0:T(1,128)S(1)} fusion(f32[16,4,1,2944]{3,2,1,0:T(1,128)S(1)} %get-tuple-element.535, s32[]{:T(128)S(6)} %select_n.276, s32[]{:T(128)S(6)} %select_n.277, s32[]{:T(128)S(6)} %select_n.278, s32[]{:T(128)S(6)} %select_n.279, s32[]{:T(128)S(6)} %select_n.280, f32[16,4,1,2880]{3,2,1,0:T(1,128)S(1)} %get-tuple-element.513, ...), kind=kLoop, calls=%fused_computation.4.clone.1 | loop fusion | flops 2027520 | bytes 5161301 | tf_op jit(solution)/shard_map/while/body/eval_jaxpr/add | solution.py:84
  264.3 115.6 %while.33 = (s32[]{:T(128)}, f32[16,4,1,2880]{3,2,1,0:T(1,128)S(1)}, f32[16,65]{0,1:T(8,128)S(1)}, f32[16,4,1,2944]{3,2,1,0:T(1,128)S(1)}, s32[]{:T(128)}, /*ind...) while((s32[]{:T(128)}, ...), condition=%wide.region_3.4_spmd.clone, body=%wide.region_2.3_spmd.clone.sunk | while | flops 2027553 | bytes 5162514 | solution.py:93
  382.4 39.4 %all_to_all.70 = f32[64,4,1,2880]{3,1,2,0:T(4,128)S(1)} all-to-all(f32[64,4,1,2880]{3,1,2,0:T(4,128)S(1)} %maximum_bitcast_fusion), channel_id=1, replica_groups=mesh['lon'=8,'lat'=16] {'lat'}, dimensions={0} | all-to-all | bytes 5898240 | tf_op jit(solution)/shard_map/all_to_all | solution.py:141
  421.9 15.9 %copy.86 = f32[4,4,16,2880]{2,1,0,3:T(4,128)} copy(f32[4,4,16,2880]{3,1,0,2:T(4,128)S(1)} %bitcast.106) | data formatting | bytes 5898240 | tf_op jit(solution)/shard_map/all_to_all | solution.py:141
  437.8 19.6 %reshape.143 = f32[8,1,92160]{2,1,0:T(1,128)S(1)} reshape(f32[2880,4,4,16]{3,2,1,0:T(4,128)} %bitcast.102) | data formatting | bytes 5898240
  457.4 43.3 %all_to_all.71 = f32[8,1,92160]{2,1,0:T(1,128)} all-to-all(f32[8,1,92160]{2,1,0:T(1,128)S(1)} %reshape.143), channel_id=1, replica_groups=mesh['lon'=8,'lat'=16] {'lon'}, dimensions={0} | all-to-all | bytes 5898240 | tf_op jit(solution)/shard_map/all_to_all | solution.py:142
  501.2 9.7 %reduce = f32[8,92160]{1,0:T(8,128)S(1)} reduce(f32[8,1,92160]{2,1,0:T(1,128)} %all_to_all.71, f32[]{:T(128)} %broadcast.173), dimensions={1}, to_apply=%all_to_all.61.reduce_sub_computation | reduce | bytes 5898244 | tf_op jit(solution)/shard_map/all_to_all | solution.py:142
  510.9 25.0 %reshape.144 = f32[2880,4,4,16]{3,2,1,0:T(4,128)} reshape(f32[8,92160]{1,0:T(8,128)S(1)} %reduce) | data formatting | bytes 5898240
  535.8 17.1 %copy.90 = f32[4,4,16,8,360]{4,2,1,0,3:T(8,128)} copy(f32[4,4,16,8,360]{2,1,0,4,3:T(4,128)} %bitcast.103) | data formatting | bytes 5898240 | tf_op jit(solution)/shard_map/all_to_all | solution.py:142
  (107 shorter events, 177.2 us)
Async XLA Ops:
  0.0 93.1 %copy-start = (f32[256]{0:T(256)S(1)}, f32[256]{0:T(256)}, u32[]{:S(2)}) copy-start(f32[256]{0:T(256)} %param.9) | copy-start | bytes 3076
  3.2 11.2 %copy-start.2 = (f32[32,4,16,360]{3,2,1,0:T(8,128)S(1)}, f32[32,4,16,360]{3,2,1,0:T(8,128)}, u32[]{:S(2)}) copy-start(f32[32,4,16,360]{3,2,1,0:T(8,128)} %param.7) | copy-start | bytes 8847364
  5.2 7.9 %collective-permute-start.1 = (f32[32,4,16,1]{0,2,3,1:T(8,128)S(1)}, f32[32,4,16,1]{0,2,3,1:T(8,128)S(1)}, u32[]{:S(2)}, u32[]{:S(2)}) collective-permute-start(f32[32,4,16,1]{0,2,3,1:T(8,128)S(1)} %copy.92), channel_id=1, source_target_pairs={{16,0},{32,16},{48,32},{64,48},{80,64},{96,80},{112,96},{0,112},{1... | collective-permute-start | bytes 24584 | tf_op jit(solution)/shard_map/ppermute | solution.py:24
  8.4 3.2 collective-permute-start
  14.5 9.6 %copy-start.3 = (f32[32,4,16,1]{3,2,0,1:T(8,128)S(1)}, f32[32,4,16,1]{3,2,0,1:T(8,128)}, u32[]{:S(2)}) copy-start(f32[32,4,16,1]{3,2,0,1:T(8,128)} %copy.73) | copy-start | bytes 24580
  14.5 9.6 %copy-start.4 = (f32[32,4,16,1]{3,2,0,1:T(8,128)S(1)}, f32[32,4,16,1]{3,2,0,1:T(8,128)}, u32[]{:S(2)}) copy-start(f32[32,4,16,1]{3,2,0,1:T(8,128)} %copy.75) | copy-start | bytes 24580
  15.6 4.7 collective-permute-start.2
  18.7 5.4 collective-permute-start.3
  83.1 9.7 %copy-start.7 = (s32[256]{0:T(256)S(1)}, s32[256]{0:T(256)}, u32[]{:S(2)}) copy-start(s32[256]{0:T(256)} %param.8) | copy-start | bytes 3076
  83.1 53.6 %all-to-all-start.1 = ((f32[4,4,16,2880]{3,1,0,2:T(4,128)}), f32[4,4,16,2880]{3,1,0,2:T(4,128)}, u32[]{:S(2)}, u32[]{:S(2)}) async-start(f32[4,4,16,2880]{3,1,0,2:T(4,128)} %copy.80), calls=%async_computation.1 | async-start | bytes 6029312 | tf_op jit(solution)/shard_map/all_to_all | solution.py:134
  140.8 0.9 copy-start.5
  379.9 1.9 copy-start.6
  535.8 17.1 %copy-start.1 = (f32[256]{0:T(256)S(1)}, f32[256]{0:T(256)}, u32[]{:S(2)}) copy-start(f32[256]{0:T(256)} %param.9) | copy-start | bytes 3076
where the time goes:
time: 562 us; the launch traced here: 553 us
  other arithmetic  247 us (44%)
  blocking collectives  128 us (23%)
  local copies, waits for them, and re-layouts  109 us (19%)
  waiting for transfers between devices  48.5 us (9%)
  starting transfers between devices  16.8 us (3%)
    add x26, other arithmetic, add_one(): total + weight[:, None, None, None] * lax.dynamic_slice_in_dim(extended,...  229 us
    unnamed x22, local copies, waits for them, and re-layouts  52.8 us
    all_to_all x1, blocking collectives, shards(): lax.all_to_all(stepped, 'lon', split_axis=0, concat_axis=3, tiled=True)  45.6 us
    all_to_all x1, blocking collectives, shards(): lax.all_to_all(damped, 'lon', split_axis=3, concat_axis=0, tiled=True)  43.3 us
    all_to_all x1, waiting for transfers between devices, shards(): lax.all_to_all(gathered, 'lat', split_axis=2, concat_axis=0, tiled=True)  42.7 us
    all_to_all x1, blocking collectives, shards(): lax.all_to_all(spread, 'lat', split_axis=0, concat_axis=2, tiled=True)  39.4 us
    all_to_all x2, local copies, waits for them, and re-layouts, shards(): lax.all_to_all(damped, 'lon', split_axis=3, concat_axis=0, tiled=True)  17.6 us
    all_to_all x1, local copies, waits for them, and re-layouts, shards(): lax.all_to_all(spread, 'lat', split_axis=0, concat_axis=2, tiled=True)  15.9 us
  transfers between devices with their start and end apart: 5, of which 4 were waited for; matrix products, arithmetic and copies ran while one was open for 1% of the time, Pallas kernels for 0%

commit v1 on v0

--- a/solution.py
+++ b/solution.py
@@ -138,7 +138,9 @@
     southern = damp_block(spread[:edge], lats[:edge])
     northern = damp_block(spread[-edge:], lats[-edge:])
     spread = jnp.concatenate([southern, spread[edge:-edge], northern], axis=0)
-    damped = lax.all_to_all(spread, "lat", split_axis=0, concat_axis=2, tiled=True)
+    parts = jnp.split(spread, lax.axis_size("lat"), axis=0)
+    got = lax.all_to_all(jnp.stack(parts), "lat", 0, 0)
+    damped = jnp.concatenate(got, axis=2)
     return lax.all_to_all(damped, "lon", split_axis=3, concat_axis=0, tiled=True)
 
 

time: 562 us -> 558 us (level)
    reshape x0 -> x1, local copies, waits for them, and re-layouts: none -> 16 us  [shards(): damped = jnp.concatenate(got, axis=2)]
    all_to_all x1 -> x0, local copies, waits for them, and re-layouts: 15.9 us -> none  [shards(): lax.all_to_all(spread, 'lat', split_axis=0, concat_axis=2, tiled=True)]
    unnamed x22 -> x28, local copies, waits for them, and re-layouts: 52.8 us -> 54.7 us
where the time goes in v1:
time: 558 us; the launch traced here: 549 us
  other arithmetic  246 us (44%)
  blocking collectives  128 us (23%)
  local copies, waits for them, and re-layouts  106 us (19%)
  waiting for transfers between devices  48.5 us (9%)
  starting transfers between devices  16.8 us (3%)
    add x26, other arithmetic, add_one(): total + weight[:, None, None, None] * lax.dynamic_slice_in_dim(extended,...  229 us
    unnamed x28, local copies, waits for them, and re-layouts  54.7 us
    all_to_all x1, blocking collectives, shards(): lax.all_to_all(stepped, 'lon', split_axis=0, concat_axis=3, tiled=True)  45.6 us
    all_to_all x1, blocking collectives, shards(): lax.all_to_all(damped, 'lon', split_axis=3, concat_axis=0, tiled=True)  43.3 us
    all_to_all x1, waiting for transfers between devices, shards(): lax.all_to_all(gathered, 'lat', split_axis=2, concat_axis=0, tiled=True)  42.7 us
    all_to_all x1, blocking collectives, shards(): got = lax.all_to_all(jnp.stack(parts), 'lat', 0, 0)  39.4 us
    all_to_all x2, local copies, waits for them, and re-layouts, shards(): lax.all_to_all(damped, 'lon', split_axis=3, concat_axis=0, tiled=True)  17.6 us
    reshape x1, local copies, waits for them, and re-layouts, shards(): damped = jnp.concatenate(got, axis=2)  16 us
  transfers between devices with their start and end apart: 5, of which 4 were waited for; matrix products, arithmetic and copies ran while one was open for 1% of the time, Pallas kernels for 0%

profile of v1, /device:TPU:1, one launch (start us, length us, event | category | flops | bytes accessed | tf_op | source)
XLA Modules:
  0.0 549.3 jit_solution(12398925958732622388)
XLA Ops:
  29.0 45.6 %all_to_all.56 = f32[32,4,16,360]{3,2,1,0:T(8,128)S(1)} all-to-all(f32[32,4,16,360]{3,2,1,0:T(8,128)S(1)} %pad_maximum_fusion.1), channel_id=1, replica_groups=mesh['lon'=8,'lat'=16] {'lon'}, dimensions={0} | all-to-all | bytes 5898240 | tf_op jit(solution)/shard_map/all_to_all | solution.py:132
  79.7 9.7 %all-to-all-start.1 = ((f32[4,4,16,2880]{3,1,0,2:T(4,128)}), f32[4,4,16,2880]{3,1,0,2:T(4,128)}, u32[]{:S(2)}, u32[]{:S(2)}) async-start(f32[4,4,16,2880]{3,1,0,2:T(4,128)} %all_to_all.43), calls=%async_computation.1 | async-start | bytes 6029312 | tf_op jit(solution)/shard_map/all_to_all | solution.py:134
  90.5 42.7 %all-to-all-done.1 = f32[4,4,16,2880]{3,1,0,2:T(4,128)} async-done(((f32[4,4,16,2880]{3,1,0,2:T(4,128)}), f32[4,4,16,2880]{3,1,0,2:T(4,128)}, u32[]{:S(2)}, u32[]{:S(2)}) %all-to-all-start.1) | async-done | bytes 2949152 | tf_op jit(solution)/shard_map/all_to_all | solution.py:134
  139.3 115.6 %while.33 = (s32[]{:T(128)}, f32[16,4,1,2880]{3,2,1,0:T(1,128)S(1)}, f32[16,65]{0,1:T(8,128)S(1)}, f32[16,4,1,2944]{3,2,1,0:T(1,128)S(1)}, s32[]{:T(128)}, /*ind...) while((s32[]{:T(128)}, ...), condition=%wide.region_3.4_spmd.clone, body=%wide.region_2.3_spmd.clone.sunk | while | flops 2027553 | bytes 5162514 | solution.py:93
  139.4 8.8 %multiply_add_fusion.5 = f32[16,4,1,2880]{3,2,1,0:T(1,128)S(1)} fusion(f32[16,4,1,2944]{3,2,1,0:T(1,128)S(1)} %get-tuple-element.511, s32[]{:T(128)S(6)} %select_n.286, s32[]{:T(128)S(6)} %select_n.287, s32[]{:T(128)S(6)} %select_n.288, s32[]{:T(128)S(6)} %select_n.289, s32[]{:T(128)S(6)} %select_n.290, ...), kind=kLoop, calls=%fused_computation.19.clone.1 | loop fusion | flops 2027520 | bytes 5161301 | tf_op jit(solution)/shard_map/while/body/eval_jaxpr/add | solution.py:84
  148.2 8.8 %multiply_add_fusion.5 = f32[16,4,1,2880]{3,2,1,0:T(1,128)S(1)} fusion(f32[16,4,1,2944]{3,2,1,0:T(1,128)S(1)} %get-tuple-element.511, s32[]{:T(128)S(6)} %select_n.286, s32[]{:T(128)S(6)} %select_n.287, s32[]{:T(128)S(6)} %select_n.288, s32[]{:T(128)S(6)} %select_n.289, s32[]{:T(128)S(6)} %select_n.290, ...), kind=kLoop, calls=%fused_computation.19.clone.1 | loop fusion | flops 2027520 | bytes 5161301 | tf_op jit(solution)/shard_map/while/body/eval_jaxpr/add | solution.py:84
  157.1 8.8 %multiply_add_fusion.5 = f32[16,4,1,2880]{3,2,1,0:T(1,128)S(1)} fusion(f32[16,4,1,2944]{3,2,1,0:T(1,128)S(1)} %get-tuple-element.511, s32[]{:T(128)S(6)} %select_n.286, s32[]{:T(128)S(6)} %select_n.287, s32[]{:T(128)S(6)} %select_n.288, s32[]{:T(128)S(6)} %select_n.289, s32[]{:T(128)S(6)} %select_n.290, ...), kind=kLoop, calls=%fused_computation.19.clone.1 | loop fusion | flops 2027520 | bytes 5161301 | tf_op jit(solution)/shard_map/while/body/eval_jaxpr/add | solution.py:84
  166.0 8.8 %multiply_add_fusion.5 = f32[16,4,1,2880]{3,2,1,0:T(1,128)S(1)} fusion(f32[16,4,1,2944]{3,2,1,0:T(1,128)S(1)} %get-tuple-element.511, s32[]{:T(128)S(6)} %select_n.286, s32[]{:T(128)S(6)} %select_n.287, s32[]{:T(128)S(6)} %select_n.288, s32[]{:T(128)S(6)} %select_n.289, s32[]{:T(128)S(6)} %select_n.290, ...), kind=kLoop, calls=%fused_computation.19.clone.1 | loop fusion | flops 2027520 | bytes 5161301 | tf_op jit(solution)/shard_map/while/body/eval_jaxpr/add | solution.py:84
  174.9 8.8 %multiply_add_fusion.5 = f32[16,4,1,2880]{3,2,1,0:T(1,128)S(1)} fusion(f32[16,4,1,2944]{3,2,1,0:T(1,128)S(1)} %get-tuple-element.511, s32[]{:T(128)S(6)} %select_n.286, s32[]{:T(128)S(6)} %select_n.287, s32[]{:T(128)S(6)} %select_n.288, s32[]{:T(128)S(6)} %select_n.289, s32[]{:T(128)S(6)} %select_n.290, ...), kind=kLoop, calls=%fused_computation.19.clone.1 | loop fusion | flops 2027520 | bytes 5161301 | tf_op jit(solution)/shard_map/while/body/eval_jaxpr/add | solution.py:84
  183.8 8.8 %multiply_add_fusion.5 = f32[16,4,1,2880]{3,2,1,0:T(1,128)S(1)} fusion(f32[16,4,1,2944]{3,2,1,0:T(1,128)S(1)} %get-tuple-element.511, s32[]{:T(128)S(6)} %select_n.286, s32[]{:T(128)S(6)} %select_n.287, s32[]{:T(128)S(6)} %select_n.288, s32[]{:T(128)S(6)} %select_n.289, s32[]{:T(128)S(6)} %select_n.290, ...), kind=kLoop, calls=%fused_computation.19.clone.1 | loop fusion | flops 2027520 | bytes 5161301 | tf_op jit(solution)/shard_map/while/body/eval_jaxpr/add | solution.py:84
  192.7 8.8 %multiply_add_fusion.5 = f32[16,4,1,2880]{3,2,1,0:T(1,128)S(1)} fusion(f32[16,4,1,2944]{3,2,1,0:T(1,128)S(1)} %get-tuple-element.511, s32[]{:T(128)S(6)} %select_n.286, s32[]{:T(128)S(6)} %select_n.287, s32[]{:T(128)S(6)} %select_n.288, s32[]{:T(128)S(6)} %select_n.289, s32[]{:T(128)S(6)} %select_n.290, ...), kind=kLoop, calls=%fused_computation.19.clone.1 | loop fusion | flops 2027520 | bytes 5161301 | tf_op jit(solution)/shard_map/while/body/eval_jaxpr/add | solution.py:84
  201.6 8.8 %multiply_add_fusion.5 = f32[16,4,1,2880]{3,2,1,0:T(1,128)S(1)} fusion(f32[16,4,1,2944]{3,2,1,0:T(1,128)S(1)} %get-tuple-element.511, s32[]{:T(128)S(6)} %select_n.286, s32[]{:T(128)S(6)} %select_n.287, s32[]{:T(128)S(6)} %select_n.288, s32[]{:T(128)S(6)} %select_n.289, s32[]{:T(128)S(6)} %select_n.290, ...), kind=kLoop, calls=%fused_computation.19.clone.1 | loop fusion | flops 2027520 | bytes 5161301 | tf_op jit(solution)/shard_map/while/body/eval_jaxpr/add | solution.py:84
  210.5 8.8 %multiply_add_fusion.5 = f32[16,4,1,2880]{3,2,1,0:T(1,128)S(1)} fusion(f32[16,4,1,2944]{3,2,1,0:T(1,128)S(1)} %get-tuple-element.511, s32[]{:T(128)S(6)} %select_n.286, s32[]{:T(128)S(6)} %select_n.287, s32[]{:T(128)S(6)} %select_n.288, s32[]{:T(128)S(6)} %select_n.289, s32[]{:T(128)S(6)} %select_n.290, ...), kind=kLoop, calls=%fused_computation.19.clone.1 | loop fusion | flops 2027520 | bytes 5161301 | tf_op jit(solution)/shard_map/while/body/eval_jaxpr/add | solution.py:84
  219.4 8.8 %multiply_add_fusion.5 = f32[16,4,1,2880]{3,2,1,0:T(1,128)S(1)} fusion(f32[16,4,1,2944]{3,2,1,0:T(1,128)S(1)} %get-tuple-element.511, s32[]{:T(128)S(6)} %select_n.286, s32[]{:T(128)S(6)} %select_n.287, s32[]{:T(128)S(6)} %select_n.288, s32[]{:T(128)S(6)} %select_n.289, s32[]{:T(128)S(6)} %select_n.290, ...), kind=kLoop, calls=%fused_computation.19.clone.1 | loop fusion | flops 2027520 | bytes 5161301 | tf_op jit(solution)/shard_map/while/body/eval_jaxpr/add | solution.py:84
  228.3 8.8 %multiply_add_fusion.5 = f32[16,4,1,2880]{3,2,1,0:T(1,128)S(1)} fusion(f32[16,4,1,2944]{3,2,1,0:T(1,128)S(1)} %get-tuple-element.511, s32[]{:T(128)S(6)} %select_n.286, s32[]{:T(128)S(6)} %select_n.287, s32[]{:T(128)S(6)} %select_n.288, s32[]{:T(128)S(6)} %select_n.289, s32[]{:T(128)S(6)} %select_n.290, ...), kind=kLoop, calls=%fused_computation.19.clone.1 | loop fusion | flops 2027520 | bytes 5161301 | tf_op jit(solution)/shard_map/while/body/eval_jaxpr/add | solution.py:84
  246.1 8.8 %multiply_add_fusion.5 = f32[16,4,1,2880]{3,2,1,0:T(1,128)S(1)} fusion(f32[16,4,1,2944]{3,2,1,0:T(1,128)S(1)} %get-tuple-element.511, s32[]{:T(128)S(6)} %select_n.286, s32[]{:T(128)S(6)} %select_n.287, s32[]{:T(128)S(6)} %select_n.288, s32[]{:T(128)S(6)} %select_n.289, s32[]{:T(128)S(6)} %select_n.290, ...), kind=kLoop, calls=%fused_computation.19.clone.1 | loop fusion | flops 2027520 | bytes 5161301 | tf_op jit(solution)/shard_map/while/body/eval_jaxpr/add | solution.py:84
  259.3 115.6 %while.32 = (s32[]{:T(128)}, f32[16,4,1,2880]{3,2,1,0:T(1,128)S(1)}, f32[16,65]{0,1:T(8,128)S(1)}, f32[16,4,1,2944]{3,2,1,0:T(1,128)S(1)}, s32[]{:T(128)}, /*ind...) while((s32[]{:T(128)}, ...), condition=%wide.region_1.2_spmd.clone, body=%wide.region_0.1_spmd.clone.sunk | while | flops 2027553 | bytes 5162514 | solution.py:93
  378.5 39.4 %all_to_all.57 = f32[16,4,4,1,2880]{4,2,1,3,0:T(4,128)S(1)} all-to-all(f32[16,4,4,1,2880]{4,2,1,3,0:T(4,128)S(1)} %bitcast.153), channel_id=1, replica_groups=mesh['lon'=8,'lat'=16] {'lat'}, dimensions={0} | all-to-all | bytes 5898240 | tf_op jit(solution)/shard_map/all_to_all | solution.py:142
  418.0 16.0 %copy.57 = f32[4,4,16,2880]{2,1,0,3:T(4,128)} copy(f32[4,4,16,2880]{3,1,0,2:T(4,128)S(1)} %bitcast.146) | data formatting | bytes 5898240 | tf_op jit(solution)/shard_map/reshape | solution.py:143
  433.9 19.6 %reshape.167 = f32[8,1,92160]{2,1,0:T(1,128)S(1)} reshape(f32[2880,4,4,16]{3,2,1,0:T(4,128)} %bitcast.143) | data formatting | bytes 5898240
  453.5 43.3 %all_to_all.58 = f32[8,1,92160]{2,1,0:T(1,128)} all-to-all(f32[8,1,92160]{2,1,0:T(1,128)S(1)} %reshape.167), channel_id=1, replica_groups=mesh['lon'=8,'lat'=16] {'lon'}, dimensions={0} | all-to-all | bytes 5898240 | tf_op jit(solution)/shard_map/all_to_all | solution.py:144
  497.3 9.7 %reduce = f32[8,92160]{1,0:T(8,128)S(1)} reduce(f32[8,1,92160]{2,1,0:T(1,128)} %all_to_all.58, f32[]{:T(128)} %broadcast.173), dimensions={1}, to_apply=%all_to_all.48.reduce_sub_computation | reduce | bytes 5898244 | tf_op jit(solution)/shard_map/all_to_all | solution.py:144
  507.0 25.0 %reshape.168 = f32[2880,4,4,16]{3,2,1,0:T(4,128)} reshape(f32[8,92160]{1,0:T(8,128)S(1)} %reduce) | data formatting | bytes 5898240
  532.0 17.1 %copy.61 = f32[4,4,16,8,360]{4,2,1,0,3:T(8,128)} copy(f32[4,4,16,8,360]{2,1,0,4,3:T(4,128)} %bitcast.144) | data formatting | bytes 5898240 | tf_op jit(solution)/shard_map/all_to_all | solution.py:144
  (111 shorter events, 173.3 us)
Async XLA Ops:
  0.0 89.6 %copy-start = (f32[256]{0:T(256)S(1)}, f32[256]{0:T(256)}, u32[]{:S(2)}) copy-start(f32[256]{0:T(256)} %param.9) | copy-start | bytes 3076
  3.2 11.2 %copy-start.2 = (f32[32,4,16,360]{3,2,1,0:T(8,128)S(1)}, f32[32,4,16,360]{3,2,1,0:T(8,128)}, u32[]{:S(2)}) copy-start(f32[32,4,16,360]{3,2,1,0:T(8,128)} %param.7) | copy-start | bytes 8847364
  5.2 7.9 %collective-permute-start.1 = (f32[32,4,16,1]{0,2,3,1:T(8,128)S(1)}, f32[32,4,16,1]{0,2,3,1:T(8,128)S(1)}, u32[]{:S(2)}, u32[]{:S(2)}) collective-permute-start(f32[32,4,16,1]{0,2,3,1:T(8,128)S(1)} %copy.63), channel_id=1, source_target_pairs={{16,0},{32,16},{48,32},{64,48},{80,64},{96,80},{112,96},{0,112},{1... | collective-permute-start | bytes 24584 | tf_op jit(solution)/shard_map/ppermute | solution.py:24
  8.4 3.2 collective-permute-start
  14.5 9.6 %copy-start.3 = (f32[32,4,16,1]{3,2,0,1:T(8,128)S(1)}, f32[32,4,16,1]{3,2,0,1:T(8,128)}, u32[]{:S(2)}) copy-start(f32[32,4,16,1]{3,2,0,1:T(8,128)} %copy.39) | copy-start | bytes 24580
  14.5 9.6 %copy-start.4 = (f32[32,4,16,1]{3,2,0,1:T(8,128)S(1)}, f32[32,4,16,1]{3,2,0,1:T(8,128)}, u32[]{:S(2)}) copy-start(f32[32,4,16,1]{3,2,0,1:T(8,128)} %copy.41) | copy-start | bytes 24580
  15.6 4.7 collective-permute-start.2
  18.7 5.4 collective-permute-start.3
  79.7 9.7 %copy-start.6 = (s32[256]{0:T(256)S(1)}, s32[256]{0:T(256)}, u32[]{:S(2)}) copy-start(s32[256]{0:T(256)} %param.8) | copy-start | bytes 3076
  79.7 53.6 %all-to-all-start.1 = ((f32[4,4,16,2880]{3,1,0,2:T(4,128)}), f32[4,4,16,2880]{3,1,0,2:T(4,128)}, u32[]{:S(2)}, u32[]{:S(2)}) async-start(f32[4,4,16,2880]{3,1,0,2:T(4,128)} %all_to_all.43), calls=%async_computation.1 | async-start | bytes 6029312 | tf_op jit(solution)/shard_map/all_to_all | solution.py:134
  134.7 0.9 copy-start.5
  532.0 17.1 %copy-start.1 = (f32[256]{0:T(256)S(1)}, f32[256]{0:T(256)}, u32[]{:S(2)}) copy-start(f32[256]{0:T(256)} %param.9) | copy-start | bytes 3076
